TPU v7x, 768 devices: a whole 4x8x12 slice. The times are simulated.
768 devices in a mesh: grp: 12 (over z), sub: 64 (over y, x, core).
Axes of the slice: x: 4, y: 8, z: 12, core: 2. Of those that a mesh axis runs over, the one named last changes fastest.
Arguments:
- basis_values: bfloat16 [12288, 256, 512], P(('grp', 'sub')), may hold values from -6 to 6
- core_density: float32 [12288, 256], P(('grp', 'sub')), may hold values from 0.3 to 3
- weights: float32 [12288, 256], P(('grp', 'sub')), may hold values from 0.00025 to 0.0045
- density_blocks: bfloat16 [1536, 128, 128], P(('grp', 'sub')), may hold values from -0.01171875 to 0.01171875
- pair_block: int32 [3072, 16], P(('grp', 'sub')), may hold values from 0 to 127, as said below
- batch_set: int32 [12288], P(('grp', 'sub')), may hold values from 0 to 3
Outputs:
- hamiltonian: float32 [1536, 128, 128], P(('grp', 'sub'))
Inputs may be any that keep to these rules, and one draw needn't show every extreme that they name: `pair_block`: entry v names stored block v % 2 of the device with index v // 2 along sub in the set's group. The 64 entries of one device's sets name blocks of each device of its group exactly 1 times.
All inputs are finite; a program needn't handle non-finite values.
Results may differ from a plain program's by a relative error of at most 0.0018.
Values may be sent and summed in bfloat16 or wider, within the bound.
No kernel may reach another device: no remote copies, remote signals or barrier semaphores. Data moves between devices by JAX's collectives and lax.ppermute only.
A program may use at most 32 MiB of HBM per device.

v0:
```python
import math

import jax
import jax.numpy as jnp
from jax import lax
from jax.sharding import PartitionSpec as P

slater_factor = (3.0 / math.pi) ** (1.0 / 3.0)
density_floor = 0.1


def body(basis_values, core_density, weights, density_blocks, pair_block, batch_set):
    sub_count = lax.axis_size("sub")
    batches, points, basis_width = basis_values.shape
    local_blocks = density_blocks.shape[0]
    tile_edge = density_blocks.shape[1]
    tile_count = basis_width // tile_edge
    set_total, pair_count = pair_block.shape
    requests = set_total * pair_count
    per_peer = requests // sub_count
    wanted = pair_block.reshape(requests)
    owner_index = wanted // local_blocks
    local_slot = wanted % local_blocks
    same_owner = owner_index[:, None] == owner_index[None, :]
    earlier = (
        jnp.arange(requests, dtype=jnp.int32)[:, None]
        > jnp.arange(requests, dtype=jnp.int32)[None, :]
    )
    before_count = jnp.sum((same_owner & earlier).astype(jnp.int32), axis=1)
    position = owner_index * per_peer + before_count
    outgoing = (
        jnp.zeros((requests,), jnp.int32).at[position].set(local_slot).reshape(sub_count, per_peer)
    )
    received = lax.all_to_all(outgoing, "sub", split_axis=0, concat_axis=0, tiled=True)
    group_blocks = lax.all_gather(density_blocks, "sub", axis=0, tiled=True)
    fetched = group_blocks[wanted]
    tile_grid = fetched.reshape(set_total, tile_count, tile_count, tile_edge, tile_edge)
    set_matrices = tile_grid.transpose(0, 1, 3, 2, 4).reshape(set_total, basis_width, basis_width)

    def batch_valence(carry, packed):
        values, set_id = packed
        mixed_rows = jnp.dot(values, set_matrices[set_id], preferred_element_type=jnp.float32)
        return (carry, jnp.sum(mixed_rows * values.astype(jnp.float32), axis=1))

    unused, valence = lax.scan(batch_valence, jnp.zeros((), jnp.float32), (basis_values, batch_set))
    density = jnp.maximum(core_density + valence, density_floor)
    charge = lax.psum(jnp.sum(weights * density), ("grp", "sub"))
    electrons = float(points * batches * lax.axis_size("grp") * sub_count // 512)
    scale_factor = jnp.cbrt(electrons / charge)
    potential = -slater_factor * jnp.cbrt(density) * weights * scale_factor

    def batch_integral(running, packed):
        values, potential_row, set_id = packed
        weighted = (potential_row[:, None] * values.astype(jnp.float32)).astype(jnp.bfloat16)
        product = lax.dot_general(
            values, weighted, (((0,), (0,)), ((), ())), preferred_element_type=jnp.float32
        )
        return (running.at[set_id].add(product), None)

    per_set, unused = lax.scan(
        batch_integral,
        jnp.zeros((set_total, basis_width, basis_width), jnp.float32),
        (basis_values, potential, batch_set),
    )
    partial_value = per_set.reshape(set_total, tile_count, tile_edge, tile_count, tile_edge)
    partial_value = (
        partial_value.transpose(0, 1, 3, 2, 4)
        .reshape(requests, tile_edge, tile_edge)
        .astype(jnp.bfloat16)
    )
    outgoing_tiles = (
        jnp.zeros_like(partial_value)
        .at[position]
        .set(partial_value)
        .reshape(sub_count, per_peer, tile_edge, tile_edge)
    )
    returned = lax.all_to_all(outgoing_tiles, "sub", split_axis=0, concat_axis=0, tiled=True)
    owned = (
        jnp.arange(local_blocks, dtype=jnp.int32)[:, None] == received.reshape(1, requests)
    ).astype(jnp.bfloat16)
    summed = jnp.dot(
        owned, returned.reshape(requests, tile_edge * tile_edge), preferred_element_type=jnp.float32
    )
    return summed.reshape(local_blocks, tile_edge, tile_edge)


def solution(mesh):
    placed = (
        P(("grp", "sub"), None, None),
        P(("grp", "sub"), None),
        P(("grp", "sub"), None),
        P(("grp", "sub"), None, None),
        P(("grp", "sub"), None),
        P(("grp", "sub")),
    )
    return jax.shard_map(
        body, mesh=mesh, in_specs=placed, out_specs=P(("grp", "sub"), None, None), check_vma=False
    )
```

profile of v0, /device:TPU:1, one launch (start us, length us, event | category | flops | bytes accessed | tf_op | source)
XLA Modules:
  0.0 494.7 jit_solution(17857883126918826711)
XLA Ops:
  10.5 14.5 %all-to-all-start = ((s32[64,1,1]{2,1,0:T(1,128)}), s32[64,1,1]{2,1,0:T(1,128)S(1)}, u32[]{:S(2)}, u32[]{:S(2)}) async-start(s32[64,1,1]{2,1,0:T(1,128)} %copy.26), calls=%async_computation | async-start | bytes 65536 | tf_op jit(solution)/shard_map/all_to_all | solution.py:34
  25.1 84.1 %all-gather.2.cloned.1.call-done = bf16[128,128,128]{2,1,0:T(8,128)(2,1)} async-done(((bf16[2,128,128]{2,1,0:T(8,128)(2,1)}), bf16[128,128,128]{2,1,0:T(8,128)(2,1)}) %all-gather.2.cloned.1.call-update) | async-done | bytes 4194320 | tf_op jit(solution)/shard_map/all_gather | solution.py:35
  109.2 3.1 gather_fusion
  112.3 3.1 copy.27
  115.4 2.8 reshape.221
  118.2 67.5 %while.21 = (s32[]{:T(128)}, f32[16,256]{1,0:T(8,128)S(1)}, bf16[16,256,512]{2,1,0:T(8,128)(2,1)}, s32[16]{0:T(128)S(1)}, bf16[4,512,512]{2,1,0:T(8,128)(2,1)S(1)}, /*index=5*/s32[]{:T(128)}, s32[]{:T(128)}, s32[]{:T(128)}) while((s32[]{:T(128)}, f32[16,256]{1,0:T(8,128)S(1)}, bf16[16,256,512]{2,1,0:T(8,128)(2,1)}, s32[16]{0:T(128)S(1)}, ...), condition=%wide.region_4.5_spmd, body=%wide.region_2.4_spmd.sunk | while | flops 134610688 | bytes 1052811 | solution.py:45
  121.0 1.4 fusion.33
  125.2 1.4 fusion.33
  129.4 1.4 fusion.33
  133.6 1.4 fusion.33
  137.8 1.4 fusion.33
  142.1 1.4 fusion.33
  146.3 1.4 fusion.33
  150.5 1.4 fusion.33
  154.7 1.4 fusion.33
  158.9 1.4 fusion.33
  163.2 1.4 fusion.33
  167.4 1.4 fusion.33
  171.6 1.4 fusion.33
  175.8 1.4 fusion.33
  180.1 1.4 fusion.33
  184.3 1.4 fusion.33
  186.5 109.3 %psum.7 = f32[]{:T(128)} all-reduce(f32[]{:T(128)} %multiply_reduce_fusion), channel_id=1, replica_groups=mesh['grp'=12,'sub'=64] {'grp','sub'}, use_global_device_ids=true, to_apply=%region_6.7 | all-reduce | flops 1 | bytes 8 | tf_op jit(solution)/shard_map/psum | solution.py:47
  296.6 2.5 broadcast_in_dim.11
  299.1 111.9 %while.22 = (s32[]{:T(128)}, f32[4,512,512]{2,1,0:T(8,128)}, s32[16]{0:T(128)S(1)}, bf16[16,256,512]{2,1,0:T(8,128)(2,1)}, f32[16,256]{1,0:T(8,128)S(1)}, /*inde...) while((s32[]{:T(128)}, f32[4,512,512]{2,1,0:T(8,128)}, s32[16]{0:T(128)S(1)}, ...), condition=%wide.region_9.10_spmd, body=%wide.region_7.9_spmd.sunk | while | flops 135135248 | bytes 2626732 | solution.py:60
  301.8 0.8 and_reduce_fusion.2
  302.6 3.5 fusion.36
  308.9 0.8 and_reduce_fusion.2
  309.7 3.5 fusion.36
  315.9 0.8 and_reduce_fusion.2
  316.6 3.5 fusion.36
  322.8 0.8 and_reduce_fusion.2
  323.6 3.5 fusion.36
  329.8 0.8 and_reduce_fusion.2
  330.6 3.5 fusion.36
  336.8 0.8 and_reduce_fusion.2
  337.6 3.5 fusion.36
  343.8 0.8 and_reduce_fusion.2
  344.6 3.5 fusion.36
  350.8 0.8 and_reduce_fusion.2
  351.6 3.5 fusion.36
  357.8 0.8 and_reduce_fusion.2
  358.6 3.5 fusion.36
  364.8 0.8 and_reduce_fusion.2
  365.6 3.5 fusion.36
  371.8 0.8 and_reduce_fusion.2
  372.6 3.5 fusion.36
  378.8 0.8 and_reduce_fusion.2
  379.6 3.5 fusion.36
  385.8 0.8 and_reduce_fusion.2
  386.6 3.5 fusion.36
  392.8 0.8 and_reduce_fusion.2
  393.6 3.5 fusion.36
  400.6 3.5 fusion.36
  407.5 3.5 fusion.36
  411.0 2.5 convert_element_type.30
  413.5 2.1 convert_element_type.31
  415.6 2.1 copy.28
  417.7 1.9 broadcast_in_dim.9
  419.6 8.6 %scatter_fusion = bf16[64,128,128]{2,1,0:T(8,128)(2,1)} fusion(bf16[64,128,128]{2,1,0:T(8,128)(2,1)} %broadcast_in_dim.9, s32[64]{0:T(128)S(1)} %get-tuple-element.96, bf16[64,128,128]{2,1,0:T(8,128)(2,1)S(1)} %bitcast.75), kind=kCustom, calls=%fused_computation.2 | custom fusion | bytes 6291712 | tf_op jit(solution)/shard_map/scatter | solution.py:74
  428.2 8.0 %all-to-all-start.1 = ((bf16[64,1,128,128]{3,2,1,0:T(8,128)(2,1)}), bf16[64,1,128,128]{3,2,1,0:T(8,128)(2,1)S(1)}, u32[]{:S(2)}, u32[]{:S(2)}) async-start(bf16[64,1,128,128]{3,2,1,0:T(8,128)(2,1)} %bitcast.19), calls=%async_computation.1 | async-start | bytes 4194304 | tf_op jit(solution)/shard_map/all_to_all | solution.py:77
  436.3 1.2 reduce.6
  437.5 48.5 %all-to-all-done.1 = bf16[64,1,128,128]{3,2,1,0:T(8,128)(2,1)S(1)} async-done(((bf16[64,1,128,128]{3,2,1,0:T(8,128)(2,1)}), bf16[64,1,128,128]{3,2,1,0:T(8,128)(2,1)S(1)}, u32[]{:S(2)}, u32[]{:S(2)}) %all-to-all-start.1) | async-done | bytes 2097184 | tf_op jit(solution)/shard_map/all_to_all | solution.py:77
  485.9 1.2 fusion.13
  (89 shorter events, 28.9 us)
Async XLA Ops:
  6.5 102.6 %all-gather.2.cloned.1.call-start = ((), (), s32[]{:S(2)}) async-start(), calls=%async_computation.2 | async-start | bytes 4259840 | tf_op jit(solution)/shard_map/all_gather | solution.py:35
  10.5 417.7 %all-to-all-start = ((s32[64,1,1]{2,1,0:T(1,128)}), s32[64,1,1]{2,1,0:T(1,128)S(1)}, u32[]{:S(2)}, u32[]{:S(2)}) async-start(s32[64,1,1]{2,1,0:T(1,128)} %copy.26), calls=%async_computation | async-start | bytes 65536 | tf_op jit(solution)/shard_map/all_to_all | solution.py:34
  115.4 2.8 copy-start.3
  118.2 67.6 %copy-start = (f32[16,256]{1,0:T(8,128)S(1)}, f32[16,256]{1,0:T(8,128)}, u32[]{:S(2)}) copy-start(f32[16,256]{1,0:T(8,128)} %param.14) | copy-start | bytes 49156
  118.2 67.6 %copy-start.1 = (f32[16,256]{1,0:T(8,128)S(1)}, f32[16,256]{1,0:T(8,128)}, u32[]{:S(2)}) copy-start(f32[16,256]{1,0:T(8,128)} %param.13) | copy-start | bytes 49156
  296.6 2.5 copy-start.2
  428.2 57.7 %all-to-all-start.1 = ((bf16[64,1,128,128]{3,2,1,0:T(8,128)(2,1)}), bf16[64,1,128,128]{3,2,1,0:T(8,128)(2,1)S(1)}, u32[]{:S(2)}, u32[]{:S(2)}) async-start(bf16[64,1,128,128]{3,2,1,0:T(8,128)(2,1)} %bitcast.19), calls=%async_computation.1 | async-start | bytes 4194304 | tf_op jit(solution)/shard_map/all_to_all | solution.py:77
Sparse Core Ops, SparseCore 0:
  11.3 97.8 all-gather.1
where the time goes:
time: 498 us; the launch traced here: 495 us
  waiting for transfers between devices  133 us (27%)
  blocking collectives  109 us (22%)
  matrix products  79.3 us (16%)
  loops' own time  66.8 us (13%)
  local copies, waits for them, and re-layouts  51.9 us (10%)
  starting transfers between devices  22.6 us (5%)
  other arithmetic  17.2 us (3%)
  between operations  14.3 us (3%)
    psum x1, blocking collectives, body(): charge = lax.psum(jnp.sum(weights * density), ('grp', 'sub'))  109 us
    all_gather x1, waiting for transfers between devices, body(): group_blocks = lax.all_gather(density_blocks, 'sub', axis=0, tiled=True)  84.1 us
    dot_general x16, matrix products, batch_integral(): lax.dot_general(values, weighted, (((0,), (0,)), ((), ())), preferred_ele...  55.4 us
    all_to_all x1, waiting for transfers between devices, body(): lax.all_to_all(outgoing_tiles, 'sub', split_axis=0, concat_axis=0, tiled=...  48.5 us
    another operation x1, loops' own time, body(): lax.scan(batch_valence, jnp.zeros((), jnp.float32), (basis_values, batch_...  33.5 us
    another operation x1, loops' own time, body(): lax.scan(batch_integral, jnp.zeros((set_total, basis_width, basis_width),...  33.3 us
    dot_general x16, matrix products, batch_valence(): jnp.dot(values, set_matrices[set_id], preferred_element_type=jnp.float32)  22.7 us
    dynamic_slice x32, local copies, waits for them, and re-layouts, body(): lax.scan(batch_valence, jnp.zeros((), jnp.float32), (basis_values, batch_...  21.2 us
  transfers between devices with their start and end apart: 3, of which 2 were waited for; matrix products, arithmetic and copies ran while one was open for 30% of the time, Pallas kernels for 0%

commit v1 on v0

v1 whole, which is shorter than its diff:
```python
import math

import jax
import jax.numpy as jnp
from jax import lax
from jax.experimental import pallas as pl
from jax.experimental.pallas import tpu as pltpu
from jax.sharding import Mesh, PartitionSpec as P

slater_factor = (3.0 / math.pi) ** (1.0 / 3.0)
density_floor = 0.1

Y, X, C = 8, 4, 2
SUB = Y * X * C
TILE = 128
TILES = 4
WIDTH = TILES * TILE
PAIRS = TILES * TILES
SETS = 4
REQUESTS = SETS * PAIRS
BATCHES = 16
POINTS = 256
LOCAL = 2
EXTRA = 16
ROWS = LOCAL * TILE + EXTRA


def cube_root(value):
    return jnp.exp2(jnp.log2(value) * (1.0 / 3.0))


def transpose_kernel(values_ref, flipped_ref):
    flipped_ref[0] = values_ref[0].T


def batch_kernel(
    pair_ref,
    set_ref,
    core_ref,
    near_ref,
    far_ref,
    values_ref,
    flipped_ref,
    core_density_ref,
    weights_ref,
    tiles_ref,
    charge_ref,
    matrices,
    valence,
    potential,
    totals,
):
    my_core = core_ref[0]
    for k in range(REQUESTS):
        wanted = pair_ref[k]
        owner = wanted // LOCAL
        slot = wanted % LOCAL
        y, x, c = owner // (X * C), (owner // C) % X, owner % C
        s, a, b = k // PAIRS, (k // TILES) % TILES, k % TILES
        rows = pl.ds(pl.multiple_of(slot * TILE, TILE), TILE)
        near = near_ref[x, y, rows, :]
        far = far_ref[x, y, rows, :]
        matrices[s, a * TILE : (a + 1) * TILE, b * TILE : (b + 1) * TILE] = jnp.where(
            c == my_core, near, far
        )

    def batch_valence(b, carry):
        flipped = flipped_ref[b]
        mixed = jnp.dot(matrices[set_ref[b]], flipped, preferred_element_type=jnp.float32)
        valence[pl.ds(b, 1), :] = jnp.sum(
            mixed * flipped.astype(jnp.float32), axis=0, keepdims=True
        )
        return carry

    lax.fori_loop(0, BATCHES, batch_valence, 0, unroll=2)
    density = jnp.maximum(core_density_ref[...] + valence[...], density_floor)
    weights = weights_ref[...]
    charge_ref[...] = jnp.broadcast_to(jnp.sum(weights * density), charge_ref.shape)
    potential[...] = -slater_factor * cube_root(density) * weights
    totals[...] = jnp.zeros_like(totals)

    def batch_integral(b, carry):
        weighted = (flipped_ref[b].astype(jnp.float32) * potential[pl.ds(b, 1), :]).astype(
            jnp.bfloat16
        )
        totals[set_ref[b]] += jnp.dot(
            weighted, values_ref[b], preferred_element_type=jnp.float32
        )
        return carry

    lax.fori_loop(0, BATCHES, batch_integral, 0, unroll=2)
    for k in range(REQUESTS):
        owner = pair_ref[k] // LOCAL
        s, a, b = k // PAIRS, (k // TILES) % TILES, k % TILES
        tiles_ref[owner] = totals[
            s, a * TILE : (a + 1) * TILE, b * TILE : (b + 1) * TILE
        ].astype(jnp.bfloat16)


def sum_kernel(electrons, slot_ref, tiles_ref, charge_ref, out_ref):
    charge = jnp.sum(charge_ref[:, 0:1, :], axis=0)
    scale = cube_root(electrons / charge)
    out_ref[...] = jnp.zeros_like(out_ref)
    for d in range(SUB):
        out_ref[slot_ref[d]] += tiles_ref[d].astype(jnp.float32)
    out_ref[...] = out_ref[...] * scale[None]


def body(basis_values, core_density, weights, density_blocks, pair_block, batch_set):
    vmem = pl.BlockSpec(memory_space=pltpu.VMEM)
    smem = pl.BlockSpec(memory_space=pltpu.SMEM)
    params = pltpu.CompilerParams(vmem_limit_bytes=56 * 1024 * 1024)
    y, x, c = lax.axis_index("y"), lax.axis_index("x"), lax.axis_index("c")
    me = (y * X + x) * C + c
    wanted = pair_block.reshape(REQUESTS)
    lanes = jnp.arange(TILE, dtype=jnp.int32)
    slots = jnp.sum(
        jnp.where((wanted // LOCAL)[:, None] == lanes[None, :], (wanted % LOCAL)[:, None], 0), axis=0
    ).astype(jnp.bfloat16)
    payload = jnp.concatenate(
        [density_blocks.reshape(LOCAL * TILE, TILE), jnp.broadcast_to(slots[None, :], (EXTRA, TILE))]
    )
    column = lax.all_to_all(
        jnp.broadcast_to(payload[None], (Y, ROWS, TILE)), "y", split_axis=0, concat_axis=0, tiled=True
    )
    near = lax.all_to_all(
        jnp.broadcast_to(column[None], (X, Y, ROWS, TILE)),
        "x",
        split_axis=0,
        concat_axis=0,
        tiled=True,
    )
    far = lax.ppermute(near, "c", [(0, 1), (1, 0)])

    flipped = pl.pallas_call(
        transpose_kernel,
        grid=(BATCHES,),
        in_specs=[pl.BlockSpec((1, POINTS, WIDTH), lambda b: (b, 0, 0))],
        out_specs=pl.BlockSpec((1, WIDTH, POINTS), lambda b: (b, 0, 0)),
        out_shape=jax.ShapeDtypeStruct((BATCHES, WIDTH, POINTS), jnp.bfloat16),
    )(basis_values)

    tiles, charge = pl.pallas_call(
        batch_kernel,
        in_specs=[smem, smem, smem, vmem, vmem, vmem, vmem, vmem, vmem],
        out_specs=[vmem, vmem],
        out_shape=[
            jax.ShapeDtypeStruct((SUB, TILE, TILE), jnp.bfloat16),
            jax.ShapeDtypeStruct((12, 8, TILE), jnp.float32),
        ],
        scratch_shapes=[
            pltpu.VMEM((SETS, WIDTH, WIDTH), jnp.bfloat16),
            pltpu.VMEM((BATCHES, POINTS), jnp.float32),
            pltpu.VMEM((BATCHES, POINTS), jnp.float32),
            pltpu.VMEM((SETS, WIDTH, WIDTH), jnp.float32),
        ],
        compiler_params=params,
    )(wanted, batch_set, c.reshape(1), near, far, basis_values, flipped, core_density, weights)

    returned = lax.all_to_all(tiles, ("y", "x", "c"), split_axis=0, concat_axis=0, tiled=True)
    column_charge = lax.all_to_all(charge, "grp", split_axis=0, concat_axis=0, tiled=True)
    column_charge = jnp.broadcast_to(jnp.sum(column_charge, axis=0)[None], (SUB, 8, TILE))
    group_charge = lax.all_to_all(
        column_charge, ("y", "x", "c"), split_axis=0, concat_axis=0, tiled=True
    )
    near_slots = near[:, :, LOCAL * TILE, :]
    far_slots = far[:, :, LOCAL * TILE, :]
    both = jnp.where(
        (c == jnp.arange(C, dtype=jnp.int32))[:, None, None, None], near_slots[None], far_slots[None]
    )
    mine = jnp.sum(jnp.where(lanes == me, both, 0), axis=-1, dtype=jnp.float32)
    slot_of = mine.transpose(2, 1, 0).reshape(SUB).astype(jnp.int32)
    electrons = float(POINTS * BATCHES * 12 * SUB // 512)

    def summed(slot_ref, tiles_ref, charge_ref, out_ref):
        sum_kernel(electrons, slot_ref, tiles_ref, charge_ref, out_ref)

    return pl.pallas_call(
        summed,
        in_specs=[smem, vmem, vmem],
        out_specs=vmem,
        out_shape=jax.ShapeDtypeStruct((LOCAL, TILE, TILE), jnp.float32),
        compiler_params=params,
    )(slot_of, returned, group_charge)


def solution(mesh):
    split = Mesh(mesh.devices.reshape(12, Y, X, C), ("grp", "y", "x", "c"))
    every = ("grp", "y", "x", "c")
    placed = (
        P(every, None, None),
        P(every, None),
        P(every, None),
        P(every, None, None),
        P(every, None),
        P(every),
    )
    return jax.shard_map(
        body, mesh=split, in_specs=placed, out_specs=P(every, None, None), check_vma=False
    )
```

time: 498 us -> 191 us (0.38)
  waiting for transfers between devices: 133 us -> 47 us
  matrix products: 79.3 us -> 0 us
  loops' own time: 66.8 us -> 0 us
  local copies, waits for them, and re-layouts: 51.9 us -> 4.95 us
  Pallas kernels: 0 us -> 29.3 us
  other arithmetic: 17.2 us -> 1.16 us
  between operations: 14.3 us -> 0.12 us
  blocking collectives: 109 us -> 96.2 us
  starting transfers between devices: 22.6 us -> 10.5 us
    psum x1 -> x0, blocking collectives: 109 us -> none  [body(): charge = lax.psum(jnp.sum(weights * density), ('grp', 'sub'))]
    all_to_all x0 -> x4, blocking collectives: none -> 96.2 us  [the longest x1 32.6 us: body(): lax.all_to_all(jnp.broadcast_to(column[None], (X, Y, ROWS, TILE)), 'x', s...]
    all_gather x1 -> x0, waiting for transfers between devices: 84.1 us -> none  [body(): group_blocks = lax.all_gather(density_blocks, 'sub', axis=0, tiled=True)]
    dot_general x33 -> x0, matrix products: 79.3 us -> none  [the longest x16 55.4 us: batch_integral(): lax.dot_general(values, weighted, (((0,), (0,)), ((), ())), preferred_ele...]
    another operation x2 -> x0, loops' own time: 66.8 us -> none  [the longest x1 33.5 us: body(): lax.scan(batch_valence, jnp.zeros((), jnp.float32), (basis_values, batch_...]
    pallas_call x0 -> x3, Pallas kernels: none -> 29.3 us  [the longest x1 15.6 us: body(): pl.pallas_call(batch_kernel, in_specs=[smem, smem, smem, vmem, vmem, vmem...]
    dynamic_slice x48 -> x0, local copies, waits for them, and re-layouts: 21.3 us -> none  [the longest x32 21.2 us: body(): lax.scan(batch_valence, jnp.zeros((), jnp.float32), (basis_values, batch_...]
    all_to_all x2 -> x1, starting transfers between devices: 22.6 us -> 4.71 us  [body(): lax.all_to_all(tiles, ('y', 'x', 'c'), split_axis=0, concat_axis=0, tiled...]
  transfers between devices with their start and end apart: 3 -> 2, of which waited for: 2 -> 1; matrix products, arithmetic and copies ran while one was open for 30% -> 1% of each run, Pallas kernels for 0% -> 6%
where the time goes in v1:
time: 191 us; the launch traced here: 189 us
  blocking collectives  96.2 us (50%)
  waiting for transfers between devices  47 us (25%)
  Pallas kernels  29.3 us (15%)
  starting transfers between devices  10.5 us (5%)
  local copies, waits for them, and re-layouts  4.95 us (3%)
    all_to_all x1, waiting for transfers between devices, body(): lax.all_to_all(tiles, ('y', 'x', 'c'), split_axis=0, concat_axis=0, tiled...  47 us
    all_to_all x1, blocking collectives, body(): lax.all_to_all(jnp.broadcast_to(column[None], (X, Y, ROWS, TILE)), 'x', s...  32.6 us
    all_to_all x1, blocking collectives, body(): lax.all_to_all(charge, 'grp', split_axis=0, concat_axis=0, tiled=True)  24.3 us
    all_to_all x1, blocking collectives, body(): lax.all_to_all(jnp.broadcast_to(payload[None], (Y, ROWS, TILE)), 'y', spl...  19.9 us
    all_to_all x1, blocking collectives, body(): lax.all_to_all(column_charge, ('y', 'x', 'c'), split_axis=0, concat_axis=...  19.4 us
    pallas_call x1, Pallas kernels, body(): pl.pallas_call(batch_kernel, in_specs=[smem, smem, smem, vmem, vmem, vmem...  15.6 us
    pallas_call x1, Pallas kernels, body(): pl.pallas_call(transpose_kernel, grid=(BATCHES,), in_specs=[pl.BlockSpec(...  10.8 us
    ppermute x1, starting transfers between devices, body(): far = lax.ppermute(near, 'c', [(0, 1), (1, 0)])  5.83 us
  transfers between devices with their start and end apart: 2, of which 1 were waited for; matrix products, arithmetic and copies ran while one was open for 1% of the time, Pallas kernels for 6%

profile of v1, /device:TPU:1, one launch (start us, length us, event | category | flops | bytes accessed | tf_op | source)
XLA Modules:
  0.0 189.3 jit_solution(11502396459100892187)
XLA Ops:
  0.0 0.8 reshape.73.pair_ref
  0.8 0.0 copy-start.2
  0.8 0.1 select_reduce_fusion
  0.9 0.8 pad_maximum_fusion
  1.7 0.1 broadcast_in_dim.81
  1.8 19.9 %all_to_all.25 = bf16[8,272,128]{2,1,0:T(8,128)(2,1)S(1)} all-to-all(bf16[8,272,128]{2,1,0:T(8,128)(2,1)S(1)} %broadcast_in_dim.81), channel_id=1, replica_groups=mesh['grp'=12,'y'=8,'x'=4,'c'=2] {'y'}, dimensions={0} | all-to-all | bytes 1114112 | tf_op jit(solution)/shard_map/all_to_all | solution.py:123
  21.8 0.3 broadcast_in_dim.82
  22.0 0.0 copy-done.2
  22.1 32.6 %all_to_all.26.near_ref = bf16[4,8,272,128]{3,2,1,0:T(8,128)(2,1)S(1)} all-to-all(bf16[4,8,272,128]{3,2,1,0:T(8,128)(2,1)S(1)} %broadcast_in_dim.82), channel_id=1, replica_groups=mesh['grp'=12,'y'=8,'x'=4,'c'=2] {'x'}, dimensions={0} | all-to-all | bytes 4456448 | tf_op jit(solution)/shard_map/all_to_all | solution.py:126
  54.6 0.0 copy-start
  54.6 5.8 %collective-permute-start = (bf16[4,8,272,128]{3,2,1,0:T(8,128)(2,1)S(1)}, bf16[4,8,272,128]{3,2,1,0:T(8,128)(2,1)}, u32[]{:S(2)}, u32[]{:S(2)}) collective-permute-start(bf16[4,8,272,128]{3,2,1,0:T(8,128)(2,1)S(1)} %all_to_all.26.near_ref), channel_id=1, source_target_pairs={{0,1},{1,0},{2,3},{3,2},{4,5},{5,4},{6,7},{7,6},{8,9},{9,8},{10,11... | collective-permute-start | bytes 6684680 | tf_op jit(solution)/shard_map/ppermute | solution.py:133
  60.5 10.8 %shard_map.64.flipped_ref = bf16[16,512,256]{2,1,0:T(8,128)(2,1)} custom-call(bf16[16,256,512]{2,1,0:T(8,128)(2,1)} %values_ref.3), custom_call_target="tpu_custom_call" | custom-call | tf_op jit(solution)/shard_map/pallas_call | solution.py:135
  71.3 0.0 copy-done
  71.3 0.0 collective-permute-done.far_ref
  71.3 15.6 %shard_map.65 = (bf16[64,128,128]{2,1,0:T(8,128)(2,1)}, f32[12,8,128]{2,1,0:T(8,128)}) custom-call(s32[64]{0:T(128)} %copy-done.2, s32[16]{0:T(128)} %set_ref.1, s32[1]{0:T(128)} %bitcast.2.core_ref, bf16[4,8,272,128]{3,2,1,0:T(8,128)(2,1)} %copy-done, bf16[4,8,272,128]{3,2,1,0:T(8,128)(2,1)} %collective-permute-done.far_ref, ...), custom_call_target="tpu_custom_call" | custom-call | tf_op jit(solution)/shard_map/pallas_call | solution.py:143
  86.9 24.3 %all_to_all.27 = f32[12,8,128]{2,1,0:T(8,128)S(1)} all-to-all(f32[12,8,128]{2,1,0:T(8,128)} %get-tuple-element.8), channel_id=1, replica_groups=mesh['grp'=12,'y'=8,'x'=4,'c'=2] {'grp'}, dimensions={0} | all-to-all | bytes 98304 | tf_op jit(solution)/shard_map/all_to_all | solution.py:161
  111.3 19.4 %all_to_all.28.charge_ref = f32[64,8,128]{2,1,0:T(8,128)} all-to-all(f32[64,8,128]{2,1,0:T(8,128)S(1)} %broadcast_in_dim.88), channel_id=1, replica_groups=mesh['grp'=12,'y'=8,'x'=4,'c'=2] {'y','x','c'}, dimensions={0} | all-to-all | bytes 524288 | tf_op jit(solution)/shard_map/all_to_all | solution.py:163
  130.7 4.7 %all-to-all-start.2 = ((bf16[64,128,128]{2,1,0:T(8,128)(2,1)}), bf16[64,128,128]{2,1,0:T(8,128)(2,1)S(1)}, u32[]{:S(2)}, u32[]{:S(2)}) async-start(bf16[64,128,128]{2,1,0:T(8,128)(2,1)} %get-tuple-element.7), calls=%async_computation.2 | async-start | bytes 4194304 | tf_op jit(solution)/shard_map/all_to_all | solution.py:160
  135.4 0.9 slice.8
  136.3 0.9 slice.9
  137.2 0.2 convert_reduce_fusion
  137.4 0.1 copy.7
  137.5 0.6 convert_element_type.23.slot_ref
  138.1 47.0 %all-to-all-done.2.tiles_ref = bf16[64,128,128]{2,1,0:T(8,128)(2,1)S(1)} async-done(((bf16[64,128,128]{2,1,0:T(8,128)(2,1)}), bf16[64,128,128]{2,1,0:T(8,128)(2,1)S(1)}, u32[]{:S(2)}, u32[]{:S(2)}) %all-to-all-start.2) | async-done | bytes 2097184 | tf_op jit(solution)/shard_map/all_to_all | solution.py:160
  185.1 0.0 copy-start.1
  185.1 1.3 copy-done.1
  186.4 2.9 %shard_map.66 = f32[2,128,128]{2,1,0:T(8,128)} custom-call(s32[64]{0:T(128)} %convert_element_type.23.slot_ref, bf16[64,128,128]{2,1,0:T(8,128)(2,1)} %copy-done.1, f32[64,8,128]{2,1,0:T(8,128)} %all_to_all.28.charge_ref), custom_call_target="tpu_custom_call" | custom-call | tf_op jit(solution)/shard_map/pallas_call | solution.py:178
  (10 shorter events, 0.1 us)
Async XLA Ops:
  0.8 21.3 %copy-start.2 = (s32[64]{0:T(128)}, s32[64]{0:T(128)S(1)}, u32[]{:S(2)}) copy-start(s32[64]{0:T(128)S(1)} %reshape.73.pair_ref) | copy-start | bytes 772
  54.6 16.7 %copy-start = (bf16[4,8,272,128]{3,2,1,0:T(8,128)(2,1)}, bf16[4,8,272,128]{3,2,1,0:T(8,128)(2,1)S(1)}, u32[]{:S(2)}) copy-start(bf16[4,8,272,128]{3,2,1,0:T(8,128)(2,1)S(1)} %all_to_all.26.near_ref) | copy-start | bytes 6684676
  54.6 16.7 %collective-permute-start = (bf16[4,8,272,128]{3,2,1,0:T(8,128)(2,1)S(1)}, bf16[4,8,272,128]{3,2,1,0:T(8,128)(2,1)}, u32[]{:S(2)}, u32[]{:S(2)}) collective-permute-start(bf16[4,8,272,128]{3,2,1,0:T(8,128)(2,1)S(1)} %all_to_all.26.near_ref), channel_id=1, source_target_pairs={{0,1},{1,0},{2,3},{3,2},{4,5},{5,4},{6,7},{7,6},{8,9},{9,8},{10,11... | collective-permute-start | bytes 6684680 | tf_op jit(solution)/shard_map/ppermute | solution.py:133
  130.7 54.4 %all-to-all-start.2 = ((bf16[64,128,128]{2,1,0:T(8,128)(2,1)}), bf16[64,128,128]{2,1,0:T(8,128)(2,1)S(1)}, u32[]{:S(2)}, u32[]{:S(2)}) async-start(bf16[64,128,128]{2,1,0:T(8,128)(2,1)} %get-tuple-element.7), calls=%async_computation.2 | async-start | bytes 4194304 | tf_op jit(solution)/shard_map/all_to_all | solution.py:160
  185.1 1.4 copy-start.1

commit v2 on v1

v2 whole, which is shorter than its diff:
```python
import math

import jax
import jax.numpy as jnp
from jax import lax
from jax.experimental import pallas as pl
from jax.experimental.pallas import tpu as pltpu
from jax.sharding import Mesh, PartitionSpec as P

slater_factor = (3.0 / math.pi) ** (1.0 / 3.0)
density_floor = 0.1

Y, X, C = 8, 4, 2
SUB = Y * X * C
TILE = 128
TILES = 4
WIDTH = TILES * TILE
PAIRS = TILES * TILES
SETS = 4
REQUESTS = SETS * PAIRS
BATCHES = 16
POINTS = 256
LOCAL = 2
ROWS = LOCAL * TILE
CHARGE_LANE = TILE - 1
GROUP = 8


def cube_root(value):
    return jnp.exp2(jnp.log2(value) * (1.0 / 3.0))


def transpose_kernel(values_ref, flipped_ref):
    for b in range(values_ref.shape[0]):
        flipped_ref[b] = values_ref[b].T


def batch_kernel(
    pair_ref,
    set_ref,
    core_ref,
    near_ref,
    far_ref,
    values_ref,
    flipped_ref,
    core_density_ref,
    weights_ref,
    tiles_ref,
    charge_ref,
    matrices,
    values,
    flipped,
    valence,
    potential,
    totals,
    rounded,
    tile_sem,
    value_sems,
    flip_sems,
    out_sem,
):
    my_core = core_ref[0]

    def fetch(source, target, sems, g):
        part = pl.ds(g * GROUP, GROUP)
        return pltpu.make_async_copy(source.at[part], target.at[part], sems.at[g])

    fetch(flipped_ref, flipped, flip_sems, 0).start()

    def fetch_tile(k, carry):
        wanted = pair_ref[k]
        owner = wanted // LOCAL
        y, x, c = owner // (X * C), (owner // C) % X, owner % C
        rows = pl.ds(pl.multiple_of((wanted % LOCAL) * TILE, TILE), TILE)
        into = matrices.at[
            k // PAIRS,
            pl.ds(pl.multiple_of((k // TILES) % TILES * TILE, TILE), TILE),
            pl.ds(pl.multiple_of(k % TILES * TILE, TILE), TILE),
        ]

        @pl.when(c == my_core)
        def _():
            pltpu.make_async_copy(near_ref.at[x, y, rows, :], into, tile_sem).start()

        @pl.when(c != my_core)
        def _():
            pltpu.make_async_copy(far_ref.at[x, y, rows, :], into, tile_sem).start()

        return carry

    lax.fori_loop(0, REQUESTS, fetch_tile, 0, unroll=8)
    for g in range(1, BATCHES // GROUP):
        fetch(flipped_ref, flipped, flip_sems, g).start()
    for g in range(BATCHES // GROUP):
        fetch(values_ref, values, value_sems, g).start()
    totals[...] = jnp.zeros_like(totals)
    pltpu.make_async_copy(matrices, matrices, tile_sem).wait()

    def group_valence(g, carry):
        fetch(flipped_ref, flipped, flip_sems, g).wait()
        for i in range(GROUP):
            b = g * GROUP + i
            turned = flipped[b]
            mixed = jnp.dot(matrices[set_ref[b]], turned, preferred_element_type=jnp.float32)
            valence[pl.ds(b, 1), :] = jnp.sum(
                mixed * turned.astype(jnp.float32), axis=0, keepdims=True
            )
        return carry

    lax.fori_loop(0, BATCHES // GROUP, group_valence, 0)
    density = jnp.maximum(core_density_ref[...] + valence[...], density_floor)
    weights = weights_ref[...]
    charge_ref[...] = jnp.broadcast_to(jnp.sum(weights * density), charge_ref.shape)
    potential[...] = -slater_factor * cube_root(density) * weights

    def group_integral(g, carry):
        fetch(values_ref, values, value_sems, g).wait()
        for i in range(GROUP):
            b = g * GROUP + i
            weighted = (flipped[b].astype(jnp.float32) * potential[pl.ds(b, 1), :]).astype(
                jnp.bfloat16
            )
            totals[set_ref[b]] += jnp.dot(
                weighted, values[b], preferred_element_type=jnp.float32
            )
        return carry

    lax.fori_loop(0, BATCHES // GROUP, group_integral, 0)
    for k in range(REQUESTS):
        s, a, b = k // PAIRS, (k // TILES) % TILES, k % TILES
        rounded[k] = totals[
            s, a * TILE : (a + 1) * TILE, b * TILE : (b + 1) * TILE
        ].astype(jnp.bfloat16)
        pltpu.make_async_copy(rounded.at[k], tiles_ref.at[pair_ref[k] // LOCAL], out_sem).start()
    pltpu.make_async_copy(rounded, tiles_ref, out_sem).wait()


def sum_kernel(electrons, me_ref, tiles_ref, rows_ref, out_ref, second):
    rows = rows_ref[...]
    charge = jnp.sum(rows[:, CHARGE_LANE:])
    scale = cube_root(jnp.full((1, TILE), electrons, jnp.float32) / charge)
    lane = lax.broadcasted_iota(jnp.int32, (TILE, TILE), 0)
    pick = (lane == me_ref[0]).astype(jnp.bfloat16)
    second[...] = jnp.dot(rows.astype(jnp.bfloat16), pick, preferred_element_type=jnp.float32)
    step = 16
    for r in range(0, TILE, step):
        sums = [jnp.zeros((step, TILE), jnp.float32), jnp.zeros((step, TILE), jnp.float32)]
        for d in range(SUB):
            tile = tiles_ref[d, r : r + step, :].astype(jnp.float32)
            in_second = jnp.broadcast_to(second[d : d + 1, :], tile.shape) > 0.5
            sums[0] += jnp.where(in_second, 0.0, tile)
            sums[1] += jnp.where(in_second, tile, 0.0)
        for slot in range(LOCAL):
            out_ref[slot, r : r + step, :] = sums[slot] * scale


def body(basis_values, core_density, weights, density_blocks, pair_block, batch_set):
    vmem = pl.BlockSpec(memory_space=pltpu.VMEM)
    smem = pl.BlockSpec(memory_space=pltpu.SMEM)
    anywhere = pl.BlockSpec(memory_space=pl.ANY)
    params = pltpu.CompilerParams(vmem_limit_bytes=56 * 1024 * 1024)

    def kept(array):
        return pltpu.with_memory_space_constraint(array, pltpu.VMEM)

    y, x, c = lax.axis_index("y"), lax.axis_index("x"), lax.axis_index("c")
    me = (y * X + x) * C + c
    wanted = pair_block.reshape(REQUESTS)
    column = lax.all_to_all(
        jnp.broadcast_to(density_blocks.reshape(1, ROWS, TILE), (Y, ROWS, TILE)),
        "y",
        split_axis=0,
        concat_axis=0,
        tiled=True,
    )
    near = lax.all_to_all(
        jnp.broadcast_to(column[None], (X, Y, ROWS, TILE)),
        "x",
        split_axis=0,
        concat_axis=0,
        tiled=True,
    )
    flipped = pl.pallas_call(
        transpose_kernel,
        grid=(BATCHES // 2,),
        in_specs=[pl.BlockSpec((2, POINTS, WIDTH), lambda b: (b, 0, 0))],
        out_specs=pl.BlockSpec((2, WIDTH, POINTS), lambda b: (b, 0, 0)),
        out_shape=jax.ShapeDtypeStruct((BATCHES, WIDTH, POINTS), jnp.bfloat16),
        compiler_params=params,
    )(basis_values)
    near, flipped = lax.optimization_barrier((near, flipped))
    far = lax.ppermute(near, "c", [(0, 1), (1, 0)])

    tiles, charge = pl.pallas_call(
        batch_kernel,
        in_specs=[smem, smem, smem, anywhere, anywhere, anywhere, anywhere, vmem, vmem],
        out_specs=[anywhere, vmem],
        out_shape=[
            jax.ShapeDtypeStruct((SUB, TILE, TILE), jnp.bfloat16),
            jax.ShapeDtypeStruct((1, TILE), jnp.float32),
        ],
        scratch_shapes=[
            pltpu.VMEM((SETS, WIDTH, WIDTH), jnp.bfloat16),
            pltpu.VMEM((BATCHES, POINTS, WIDTH), jnp.bfloat16),
            pltpu.VMEM((BATCHES, WIDTH, POINTS), jnp.bfloat16),
            pltpu.VMEM((BATCHES, POINTS), jnp.float32),
            pltpu.VMEM((BATCHES, POINTS), jnp.float32),
            pltpu.VMEM((SETS, WIDTH, WIDTH), jnp.float32),
            pltpu.VMEM((REQUESTS, TILE, TILE), jnp.bfloat16),
            pltpu.SemaphoreType.DMA,
            pltpu.SemaphoreType.DMA((BATCHES // GROUP,)),
            pltpu.SemaphoreType.DMA((BATCHES // GROUP,)),
            pltpu.SemaphoreType.DMA,
        ],
        compiler_params=params,
    )(
        wanted,
        batch_set,
        c.reshape(1),
        near,
        far,
        basis_values,
        flipped,
        core_density,
        weights,
    )

    returned = lax.all_to_all(tiles, ("y", "x", "c"), split_axis=0, concat_axis=0, tiled=True)
    lanes = jnp.arange(TILE, dtype=jnp.int32)
    slots = jnp.sum(
        jnp.where((wanted // LOCAL)[:, None] == lanes[None, :], (wanted % LOCAL)[:, None], 0), axis=0
    ).astype(jnp.float32)
    charge = lax.psum(charge, "grp")
    row = jnp.where(lanes[None, :] == CHARGE_LANE, charge, slots[None, :])
    rows = lax.all_gather(row, ("y", "x", "c"), axis=0, tiled=True)
    electrons = float(POINTS * BATCHES * 12 * SUB // 512)

    def summed(me_ref, tiles_ref, rows_ref, out_ref, second):
        sum_kernel(electrons, me_ref, tiles_ref, rows_ref, out_ref, second)

    return pl.pallas_call(
        summed,
        in_specs=[smem, vmem, vmem],
        out_specs=vmem,
        out_shape=jax.ShapeDtypeStruct((LOCAL, TILE, TILE), jnp.float32),
        scratch_shapes=[pltpu.VMEM((SUB, TILE), jnp.float32)],
        compiler_params=params,
    )(me.reshape(1), kept(returned), rows)


def solution(mesh):
    split = Mesh(mesh.devices.reshape(12, Y, X, C), ("grp", "y", "x", "c"))
    every = ("grp", "y", "x", "c")
    placed = (
        P(every, None, None),
        P(every, None),
        P(every, None),
        P(every, None, None),
        P(every, None),
        P(every),
    )
    return jax.shard_map(
        body, mesh=split, in_specs=placed, out_specs=P(every, None, None), check_vma=False
    )
```

time: 191 us -> 161 us (0.84)
  waiting for transfers between devices: 47 us -> 19.7 us
  Pallas kernels: 29.3 us -> 20.3 us
  starting transfers between devices: 10.5 us -> 17.9 us
  blocking collectives: 96.2 us -> 98.5 us
    all_to_all x4 -> x1, blocking collectives: 96.2 us -> 19.7 us  [body(): lax.all_to_all(jnp.broadcast_to(density_blocks.reshape(1, ROWS, TILE), (Y...]
    all_gather x0 -> x1, blocking collectives: none -> 49.3 us  [body(): rows = lax.all_gather(row, ('y', 'x', 'c'), axis=0, tiled=True)]
    all_to_all x1, waiting for transfers between devices: 47 us -> 0.01 us  [body(): lax.all_to_all(tiles, ('y', 'x', 'c'), split_axis=0, concat_axis=0, tiled...]
    psum x0 -> x1, blocking collectives: none -> 29.6 us  [body(): charge = lax.psum(charge, 'grp')]
    all_to_all x0 -> x1, waiting for transfers between devices: none -> 16.4 us  [body(): lax.all_to_all(jnp.broadcast_to(column[None], (X, Y, ROWS, TILE)), 'x', s...]
    pallas_call x2, Pallas kernels: 26.5 us -> 17.9 us  [the longest x1 10.7 us: body(): pl.pallas_call(batch_kernel, in_specs=[smem, smem, smem, anywhere, anywhe...]
    all_to_all x0 -> x1, starting transfers between devices: none -> 7.8 us  [body(): lax.all_to_all(jnp.broadcast_to(column[None], (X, Y, ROWS, TILE)), 'x', s...]
    ppermute x1, waiting for transfers between devices: 0.01 us -> 3.28 us  [body(): far = lax.ppermute(near, 'c', [(0, 1), (1, 0)])]
  transfers between devices with their start and end apart: 2 -> 3, of which waited for: 1 -> 2; matrix products, arithmetic and copies ran while one was open for 1% -> 0% of each run, Pallas kernels for 6% -> 4%
where the time goes in v2:
time: 161 us; the launch traced here: 160 us
  blocking collectives  98.5 us (61%)
  Pallas kernels  20.3 us (13%)
  waiting for transfers between devices  19.7 us (12%)
  starting transfers between devices  17.9 us (11%)
  local copies, waits for them, and re-layouts  3.32 us (2%)
    all_gather x1, blocking collectives, body(): rows = lax.all_gather(row, ('y', 'x', 'c'), axis=0, tiled=True)  49.3 us
    psum x1, blocking collectives, body(): charge = lax.psum(charge, 'grp')  29.6 us
    all_to_all x1, blocking collectives, body(): lax.all_to_all(jnp.broadcast_to(density_blocks.reshape(1, ROWS, TILE), (Y...  19.7 us
    all_to_all x1, waiting for transfers between devices, body(): lax.all_to_all(jnp.broadcast_to(column[None], (X, Y, ROWS, TILE)), 'x', s...  16.4 us
    pallas_call x1, Pallas kernels, body(): pl.pallas_call(batch_kernel, in_specs=[smem, smem, smem, anywhere, anywhe...  10.7 us
    all_to_all x1, starting transfers between devices, body(): lax.all_to_all(jnp.broadcast_to(column[None], (X, Y, ROWS, TILE)), 'x', s...  7.8 us
    pallas_call x1, Pallas kernels, body(): pl.pallas_call(transpose_kernel, grid=(BATCHES // 2,), in_specs=[pl.Block...  7.19 us
    ppermute x1, starting transfers between devices, body(): far = lax.ppermute(near, 'c', [(0, 1), (1, 0)])  5.56 us
  transfers between devices with their start and end apart: 3, of which 2 were waited for; matrix products, arithmetic and copies ran while one was open for 0% of the time, Pallas kernels for 4%

profile of v2, /device:TPU:1, one launch (start us, length us, event | category | flops | bytes accessed | tf_op | source)
XLA Modules:
  0.0 159.9 jit_solution(10769033340245195346)
XLA Ops:
  0.0 0.9 broadcast_in_dim.19
  0.9 19.7 %all_to_all.15 = bf16[8,256,128]{2,1,0:T(8,128)(2,1)S(1)} all-to-all(bf16[8,256,128]{2,1,0:T(8,128)(2,1)S(1)} %broadcast_in_dim.19), channel_id=1, replica_groups=mesh['grp'=12,'y'=8,'x'=4,'c'=2] {'y'}, dimensions={0} | all-to-all | bytes 1048576 | tf_op jit(solution)/shard_map/all_to_all | solution.py:169
  20.6 1.8 %broadcast_in_dim.32 = bf16[4,8,256,128]{3,2,1,0:T(8,128)(2,1)} broadcast(bf16[8,256,128]{2,1,0:T(8,128)(2,1)S(1)} %all_to_all.15), dimensions={1,2,3} | broadcast | bytes 2621440 | tf_op jit(solution)/shard_map/broadcast_in_dim | solution.py:177
  22.4 7.8 %all-to-all-start.1 = ((bf16[4,8,256,128]{3,2,1,0:T(8,128)(2,1)}), bf16[4,8,256,128]{3,2,1,0:T(8,128)(2,1)S(1)}, u32[]{:S(2)}, u32[]{:S(2)}) async-start(bf16[4,8,256,128]{3,2,1,0:T(8,128)(2,1)} %broadcast_in_dim.32), calls=%async_computation.1 | async-start | bytes 4194304 | tf_op jit(solution)/shard_map/all_to_all | solution.py:176
  30.2 0.0 copy-start.2
  30.2 7.2 %shard_map.64.flipped_ref = bf16[16,512,256]{2,1,0:T(8,128)(2,1)} custom-call(bf16[16,256,512]{2,1,0:T(8,128)(2,1)} %values_ref.3), custom_call_target="tpu_custom_call" | custom-call | tf_op jit(solution)/shard_map/pallas_call | solution.py:183
  37.4 16.4 %all-to-all-done.1.near_ref = bf16[4,8,256,128]{3,2,1,0:T(8,128)(2,1)S(1)} async-done(((bf16[4,8,256,128]{3,2,1,0:T(8,128)(2,1)}), bf16[4,8,256,128]{3,2,1,0:T(8,128)(2,1)S(1)}, u32[]{:S(2)}, u32[]{:S(2)}) %all-to-all-start.1) | async-done | bytes 2097184 | tf_op jit(solution)/shard_map/all_to_all | solution.py:176
  53.8 0.0 copy-start
  53.8 5.6 %collective-permute-start = (bf16[4,8,256,128]{3,2,1,0:T(8,128)(2,1)S(1)}, bf16[4,8,256,128]{3,2,1,0:T(8,128)(2,1)}, u32[]{:S(2)}, u32[]{:S(2)}) collective-permute-start(bf16[4,8,256,128]{3,2,1,0:T(8,128)(2,1)S(1)} %all-to-all-done.1.near_ref), channel_id=1, source_target_pairs={{0,1},{1,0},{2,3},{3,2},{4,5},{5,4},{6,7},{7,6},{8,9},{9,8},{10,11... | collective-permute-start | bytes 6291464 | tf_op jit(solution)/shard_map/ppermute | solution.py:192
  59.4 0.0 copy-done.2
  59.4 0.6 reshape.78.pair_ref
  60.0 3.3 %collective-permute-done.far_ref = bf16[4,8,256,128]{3,2,1,0:T(8,128)(2,1)} collective-permute-done((bf16[4,8,256,128]{3,2,1,0:T(8,128)(2,1)S(1)}, bf16[4,8,256,128]{3,2,1,0:T(8,128)(2,1)}, u32[]{:S(2)}, u32[]{:S(2)}) %collective-permute-start) | collective-permute-done | bytes 2097184 | tf_op jit(solution)/shard_map/ppermute | solution.py:192
  63.3 0.0 copy-done
  63.3 10.7 %shard_map.65 = (bf16[64,128,128]{2,1,0:T(8,128)(2,1)}, f32[1,128]{1,0:T(1,128)}) custom-call(s32[64]{0:T(128)} %reshape.78.pair_ref, s32[16]{0:T(128)} %set_ref.1, s32[1]{0:T(128)} %bitcast.1.core_ref, bf16[4,8,256,128]{3,2,1,0:T(8,128)(2,1)} %copy-done, bf16[4,8,256,128]{3,2,1,0:T(8,128)(2,1)} %collective-permute-done.far_ref, ...), custom_call_target="tpu_custom_call" | custom-call | tf_op jit(solution)/shard_map/pallas_call | solution.py:194
  74.0 0.0 copy-start.1
  74.0 0.0 copy-start.3
  74.0 4.5 %all-to-all-start.2 = ((bf16[64,128,128]{2,1,0:T(8,128)(2,1)}), bf16[64,128,128]{2,1,0:T(8,128)(2,1)S(1)}, u32[]{:S(2)}, u32[]{:S(2)}) async-start(bf16[64,128,128]{2,1,0:T(8,128)(2,1)} %get-tuple-element.11), calls=%async_computation.2 | async-start | bytes 4194304 | tf_op jit(solution)/shard_map/all_to_all | solution.py:228
  78.6 0.0 copy-done.1
  78.6 0.1 select_reduce_fusion
  78.7 0.0 copy-done.3
  78.7 29.6 %psum.7 = f32[1,128]{1,0:T(1,128)S(1)} all-reduce(f32[1,128]{1,0:T(1,128)S(1)} %copy-done.3), channel_id=1, replica_groups=mesh['grp'=12,'y'=8,'x'=4,'c'=2] {'grp'}, use_global_device_ids=true, to_apply=%region_0.1 | all-reduce | flops 128 | bytes 1024 | tf_op jit(solution)/shard_map/psum | solution.py:233
  108.3 49.3 %all-gather = f32[64,1,128]{2,1,0:T(1,128)} all-gather(f32[1,1,128]{2,1,0:T(1,128)S(1)} %fusion), channel_id=1, replica_groups=mesh['grp'=12,'y'=8,'x'=4,'c'=2] {'y','x','c'}, dimensions={0}, use_global_device_ids=true | all-gather | bytes 33280 | tf_op jit(solution)/shard_map/all_gather | solution.py:235
  157.6 0.0 all-to-all-done.2.tiles_ref
  157.6 2.3 %shard_map.66 = f32[2,128,128]{2,1,0:T(8,128)} custom-call(s32[1]{0:T(128)} %bitcast.me_ref, bf16[64,128,128]{2,1,0:T(8,128)(2,1)S(1)} %all-to-all-done.2.tiles_ref, f32[64,128]{1,0:T(8,128)} %bitcast.8), custom_call_target="tpu_custom_call" | custom-call | tf_op jit(solution)/shard_map/pallas_call | solution.py:241
  (2 shorter events, 0.0 us)
Async XLA Ops:
  22.4 31.4 %all-to-all-start.1 = ((bf16[4,8,256,128]{3,2,1,0:T(8,128)(2,1)}), bf16[4,8,256,128]{3,2,1,0:T(8,128)(2,1)S(1)}, u32[]{:S(2)}, u32[]{:S(2)}) async-start(bf16[4,8,256,128]{3,2,1,0:T(8,128)(2,1)} %broadcast_in_dim.32), calls=%async_computation.1 | async-start | bytes 4194304 | tf_op jit(solution)/shard_map/all_to_all | solution.py:176
  30.2 29.2 %copy-start.2 = (s32[4,16]{1,0:T(4,128)S(1)}, s32[4,16]{1,0:T(4,128)}, u32[]{:S(2)}) copy-start(s32[4,16]{1,0:T(4,128)} %param.10) | copy-start | bytes 772
  53.8 9.5 %copy-start = (bf16[4,8,256,128]{3,2,1,0:T(8,128)(2,1)}, bf16[4,8,256,128]{3,2,1,0:T(8,128)(2,1)S(1)}, u32[]{:S(2)}) copy-start(bf16[4,8,256,128]{3,2,1,0:T(8,128)(2,1)S(1)} %all-to-all-done.1.near_ref) | copy-start | bytes 6291460
  53.8 9.5 %collective-permute-start = (bf16[4,8,256,128]{3,2,1,0:T(8,128)(2,1)S(1)}, bf16[4,8,256,128]{3,2,1,0:T(8,128)(2,1)}, u32[]{:S(2)}, u32[]{:S(2)}) collective-permute-start(bf16[4,8,256,128]{3,2,1,0:T(8,128)(2,1)S(1)} %all-to-all-done.1.near_ref), channel_id=1, source_target_pairs={{0,1},{1,0},{2,3},{3,2},{4,5},{5,4},{6,7},{7,6},{8,9},{9,8},{10,11... | collective-permute-start | bytes 6291464 | tf_op jit(solution)/shard_map/ppermute | solution.py:192
  74.0 4.5 %copy-start.1 = (s32[64]{0:T(128)S(1)}, s32[64]{0:T(128)}, u32[]{:S(2)}) copy-start(s32[64]{0:T(128)} %reshape.78.pair_ref) | copy-start | bytes 772
  74.0 4.7 %copy-start.3 = (f32[1,128]{1,0:T(1,128)S(1)}, f32[1,128]{1,0:T(1,128)}, u32[]{:S(2)}) copy-start(f32[1,128]{1,0:T(1,128)} %get-tuple-element.12) | copy-start | bytes 1540
  74.0 83.5 %all-to-all-start.2 = ((bf16[64,128,128]{2,1,0:T(8,128)(2,1)}), bf16[64,128,128]{2,1,0:T(8,128)(2,1)S(1)}, u32[]{:S(2)}, u32[]{:S(2)}) async-start(bf16[64,128,128]{2,1,0:T(8,128)(2,1)} %get-tuple-element.11), calls=%async_computation.2 | async-start | bytes 4194304 | tf_op jit(solution)/shard_map/all_to_all | solution.py:228
